TPU v7x, 32 devices: a whole 2x2x4 slice. The times are simulated.
32 devices in a mesh: seq: 8 (over z, x), head: 4 (over y, core).
Axes of the slice: x: 2, y: 2, z: 4, core: 2. Of those that a mesh axis runs over, the one named last changes fastest.
Arguments:
- features: bfloat16 [1024, 4096], P('seq', 'head'), may hold values from -6 to 6
- proj_weight: bfloat16 [4096, 4096], P(None, 'head'), may hold values from -0.09375 to 0.09375
- query_vectors: bfloat16 [1024, 4096], P('seq', 'head'), may hold values from -6 to 6
- key_vectors: bfloat16 [1024, 4096], P('seq', 'head'), may hold values from -6 to 6
Outputs:
- rotated_queries: bfloat16 [1024, 4096], P('seq', 'head')
- rotated_keys: bfloat16 [1024, 4096], P('seq', 'head')
All inputs are finite; a program needn't handle non-finite values.
Results may differ from a plain program's by a relative error of at most 0.0024.
Values may be sent and summed in bfloat16 or wider, within the bound.
A program may use at most 128 MiB of HBM per device.

v0:
```python
import jax
import jax.numpy as jnp
from jax import lax
from jax.sharding import PartitionSpec as P

HEAD_DIM = 128


def entering(array, axis, combine, identity):
    count, place = (lax.axis_size(axis), lax.axis_index(axis))
    everything = lax.all_gather(array, axis)
    start = jnp.broadcast_to(jnp.asarray(identity, array.dtype), array.shape)

    def turn(k, before):
        reached = k < place
        new = combine(before, everything[k])
        return jnp.where(reached, new, before)

    return lax.fori_loop(0, count, turn, start)


def small_inverse(matrix):
    highest = lax.Precision.HIGHEST
    size = matrix.shape[-1]
    position = jnp.arange(size)
    strict = (position[:, None] < position[None, :]).astype(jnp.float32)
    eye_block = jnp.eye(size, dtype=jnp.float32)
    power = -2.0 * matrix * strict[None]
    result = eye_block[None] + power
    reach = 2
    while reach < size:
        power = jnp.einsum("hij,hjk->hik", power, power, precision=highest)
        result = result + jnp.einsum("hij,hjk->hik", result, power, precision=highest)
        reach = reach * 2
    return 2.0 * result


def triangle_inverse(matrix):
    highest = lax.Precision.HIGHEST
    size = matrix.shape[-1]
    if size <= 16:
        return small_inverse(matrix)
    half = size // 2
    first = triangle_inverse(matrix[:, :half, :half])
    second = triangle_inverse(matrix[:, half:, half:])
    coupling = matrix[:, :half, half:]
    middle = jnp.einsum("hij,hjk->hik", first, coupling, precision=highest)
    corner = -jnp.einsum("hij,hjk->hik", middle, second, precision=highest)
    lower_left = jnp.zeros((matrix.shape[0], size - half, half), jnp.float32)
    top = jnp.concatenate([first, corner], axis=2)
    bottom = jnp.concatenate([lower_left, second], axis=2)
    return jnp.concatenate([top, bottom], axis=1)


def upper_solve(matrix, right_side):
    highest = lax.Precision.HIGHEST
    rows = matrix.shape[1]
    size = min(128, rows)
    count = rows // size
    solved_blocks = []
    for i in reversed(range(count)):
        inverse_block = triangle_inverse(matrix)
        solved_blocks.append(
            jnp.einsum("hij,hjk->hik", inverse_block, right_side, precision=highest)
        )
    return jnp.concatenate(solved_blocks[::-1], axis=1)


def body(features, proj_weight, query_vectors, key_vectors):
    highest = lax.Precision.HIGHEST
    tok_rows = query_vectors.shape[0]
    width = proj_weight.shape[1]
    local_heads = width // HEAD_DIM
    raw_proj = jnp.dot(
        lax.all_gather(features, "head", axis=1, tiled=True),
        proj_weight,
        preferred_element_type=jnp.float32,
    )
    raw_proj = raw_proj.reshape(tok_rows, local_heads, HEAD_DIM)
    directions = raw_proj * lax.rsqrt(jnp.sum(raw_proj * raw_proj, axis=-1, keepdims=True) + 1e-06)
    reflectors = jnp.transpose(directions, (1, 0, 2))
    targets = jnp.concatenate(
        [
            query_vectors.reshape(tok_rows, local_heads, HEAD_DIM),
            key_vectors.reshape(tok_rows, local_heads, HEAD_DIM),
        ],
        axis=0,
    )
    targets = jnp.transpose(targets.astype(jnp.float32), (1, 0, 2))
    gram = jnp.einsum("hid,hjd->hij", reflectors, reflectors, precision=highest)
    position = jnp.arange(tok_rows)
    upper = (position[:, None] < position[None, :]).astype(jnp.float32)
    identity_tok = jnp.eye(tok_rows, dtype=jnp.float32)
    inverse_t = gram * upper[None] + 0.5 * identity_tok[None]
    projected = jnp.einsum("hid,htd->hit", reflectors, targets, precision=highest)
    target_pos = jnp.concatenate([position, position])
    keep = (position[:, None] <= target_pos[None, :]).astype(jnp.float32)
    masked = projected * keep[None]
    right_side = jnp.concatenate([masked, reflectors], axis=2)
    solved = upper_solve(inverse_t, right_side)
    weights_tok = solved[:, :, : 2 * tok_rows]
    factor = solved[:, :, 2 * tok_rows :]
    local_part = targets - jnp.einsum("hit,hid->htd", weights_tok, reflectors, precision=highest)
    identity = jnp.broadcast_to(
        jnp.eye(HEAD_DIM, dtype=jnp.float32), (local_heads, HEAD_DIM, HEAD_DIM)
    )
    block_product = identity - jnp.einsum("hid,hie->hde", reflectors, factor, precision=highest)

    def combine(earlier, later):
        return jnp.einsum("hde,hef->hdf", earlier, later, precision=highest)

    carried = entering(block_product, "seq", combine, identity)
    rotated = jnp.einsum("hde,hte->htd", carried, local_part, precision=highest)
    rotated = jnp.transpose(rotated, (1, 0, 2))
    rotated_queries = rotated[:tok_rows].reshape(tok_rows, width).astype(jnp.bfloat16)
    rotated_keys = rotated[tok_rows:].reshape(tok_rows, width).astype(jnp.bfloat16)
    return (rotated_queries, rotated_keys)


def solution(mesh):
    in_specs = (P("seq", "head"), P(None, "head"), P("seq", "head"), P("seq", "head"))
    out_specs = (P("seq", "head"), P("seq", "head"))
    return jax.shard_map(body, mesh=mesh, in_specs=in_specs, out_specs=out_specs, check_vma=False)
```

profile of v0, /device:TPU:0, one launch (start us, length us, event | category | flops | bytes accessed | tf_op | source)
XLA Modules:
  0.0 155.5 jit_solution(11433257053799910114)
XLA Ops:
  7.2 0.7 all-gather.4.cloned.1.call-update
  7.9 1.1 copy.38
  9.3 1.1 copy.39
  10.7 18.3 %all-gather.4.cloned.1.call-done = bf16[128,4096]{1,0:T(8,128)(2,1)} async-done(((bf16[128,1024]{1,0:T(8,128)(2,1)}), bf16[128,4096]{1,0:T(8,128)(2,1)}) %all-gather.4.cloned.1.call-update) | async-done | bytes 1048592 | tf_op jit(solution)/shard_map/all_gather | solution.py:75
  29.0 5.0 %fusion.124 = f32[128,1024]{1,0:T(8,128)S(1)} fusion(bf16[128,4096]{1,0:T(8,128)(2,1)} %all-gather.4.cloned.1.call-done, bf16[4096,1024]{1,0:T(8,128)(2,1)} %param.7), kind=kOutput, calls=%fused_computation.185 | convolution fusion | flops 1073741824 | bytes 9961472 | tf_op jit(solution)/shard_map/dot_general | solution.py:74
  34.6 1.2 fusion.9
  35.8 0.3 fusion.89
  36.1 0.3 fusion.88
  38.1 0.3 fusion.86
  39.5 0.3 fusion.84
  40.3 0.3 fusion.83
  48.6 0.3 fusion.48
  49.3 0.3 fusion.50
  50.0 0.5 fusion.35
  50.5 0.4 convolution_negate_fusion
  50.9 0.6 convolution_multiply_fusion
  51.5 1.7 %fusion.4 = f32[8,128,384]{2,1,0:T(8,128)S(1)} fusion(f32[8,128,128]{2,1,0:T(8,128)S(1)} %fusion.19, f32[8,128,256]{2,1,0:T(8,128)S(1)} %convolution_multiply_fusion, f32[8,64,64]{2,1,0:T(8,128)S(1)} %select_maximum_fusion.2, f32[8,64,64]{2,1,0:T(8,128)S(1)} %convolution_negate_fusion, f32[8,32,64]{2,1,0:T(8,128)S(1)} %concatenate.80, ...), kind=kOutput, calls=%fused_computation.5 | convolution fusion | flops 605421568 | bytes 3538944 | tf_op jit(solution)/shard_map/hij,hjk->hik/dot_general | solution.py:64
  53.2 1.8 %convolution_subtract_fusion.1 = f32[8,128,128]{2,1,0:T(8,128)} fusion(f32[8,128,128]{2,1,0:T(8,128)S(1)} %fusion.19, f32[8,128,384]{2,1,0:T(8,128)S(1)} %fusion.4, f32[128,128]{1,0:T(8,128)S(1)} %fusion.79), kind=kOutput, calls=%fused_computation.13 | convolution fusion | flops 201457664 | bytes 1638400 | tf_op jit(solution)/shard_map/hid,hie->hde/dot_general | solution.py:107
  55.2 2.9 %convolution_subtract_fusion = f32[8,256,128]{2,1,0:T(8,128)S(1)} fusion(f32[8,128,128]{2,1,0:T(8,128)S(1)} %fusion.19, f32[8,128,384]{2,1,0:T(8,128)S(1)} %fusion.4, bf16[128,8,128]{2,0,1:T(8,128)(2,1)} %copy-done, bf16[128,8,128]{2,0,1:T(8,128)(2,1)S(1)} %copy.40), kind=kOutput, calls=%fused_computation.9 | convolution fusion | flops 404226048 | bytes 3145728 | tf_op jit(solution)/shard_map/hit,hid->htd/dot_general | solution.py:103
  58.1 70.6 %all-gather.6.cloned.1.call-done = f32[64,128,128]{2,1,0:T(8,128)} async-done(((f32[8,128,128]{2,1,0:T(8,128)}), f32[64,128,128]{2,1,0:T(8,128)}) %all-gather.6.cloned.1.call-update) | async-done | bytes 4194320 | tf_op jit(solution)/shard_map/all_gather | solution.py:11
  128.7 17.1 %while.13 = (s32[]{:T(128)}, f32[8,128,128]{1,2,0:T(8,128)S(1)}, s32[]{:T(128)}, f32[8,8,128,128]{3,2,1,0:T(8,128)}, s32[]{:T(128)}) while((s32[]{:T(128)}, f32[8,128,128]{1,2,0:T(8,128)S(1)}, s32[]{:T(128)}, f32[8,8,128,128]{3,2,1,0:T(8,128)}, s32[]{:T(128)}) %tuple.48), condition=%wide.region_2.3_spmd, body=%wide.region_1.2_spmd.sunk | while | flops 201457664 | bytes 3145811 | solution.py:19
  128.7 2.1 %fusion.247 = f32[8,128,128]{1,2,0:T(8,128)S(1)} fusion(f32[8,128,128]{1,2,0:T(8,128)S(1)} %copy.69, f32[8,8,128,128]{3,2,1,0:T(8,128)} %get-tuple-element.154, s32[]{:T(128)S(6)} %copy.62, pred[]{:T(512)S(6)} %lt.168), kind=kOutput, calls=%fused_computation.1.clone.1 | convolution fusion | flops 201457664 | bytes 2097157 | tf_op jit(solution)/shard_map/while/body/eval_jaxpr/hde,hef->hdf/dot_general | solution.py:110
  130.9 2.1 %fusion.247 = f32[8,128,128]{1,2,0:T(8,128)S(1)} fusion(f32[8,128,128]{1,2,0:T(8,128)S(1)} %copy.69, f32[8,8,128,128]{3,2,1,0:T(8,128)} %get-tuple-element.154, s32[]{:T(128)S(6)} %copy.62, pred[]{:T(512)S(6)} %lt.168), kind=kOutput, calls=%fused_computation.1.clone.1 | convolution fusion | flops 201457664 | bytes 2097157 | tf_op jit(solution)/shard_map/while/body/eval_jaxpr/hde,hef->hdf/dot_general | solution.py:110
  133.0 2.1 %fusion.247 = f32[8,128,128]{1,2,0:T(8,128)S(1)} fusion(f32[8,128,128]{1,2,0:T(8,128)S(1)} %copy.69, f32[8,8,128,128]{3,2,1,0:T(8,128)} %get-tuple-element.154, s32[]{:T(128)S(6)} %copy.62, pred[]{:T(512)S(6)} %lt.168), kind=kOutput, calls=%fused_computation.1.clone.1 | convolution fusion | flops 201457664 | bytes 2097157 | tf_op jit(solution)/shard_map/while/body/eval_jaxpr/hde,hef->hdf/dot_general | solution.py:110
  135.1 2.1 %fusion.247 = f32[8,128,128]{1,2,0:T(8,128)S(1)} fusion(f32[8,128,128]{1,2,0:T(8,128)S(1)} %copy.69, f32[8,8,128,128]{3,2,1,0:T(8,128)} %get-tuple-element.154, s32[]{:T(128)S(6)} %copy.62, pred[]{:T(512)S(6)} %lt.168), kind=kOutput, calls=%fused_computation.1.clone.1 | convolution fusion | flops 201457664 | bytes 2097157 | tf_op jit(solution)/shard_map/while/body/eval_jaxpr/hde,hef->hdf/dot_general | solution.py:110
  137.3 2.1 %fusion.247 = f32[8,128,128]{1,2,0:T(8,128)S(1)} fusion(f32[8,128,128]{1,2,0:T(8,128)S(1)} %copy.69, f32[8,8,128,128]{3,2,1,0:T(8,128)} %get-tuple-element.154, s32[]{:T(128)S(6)} %copy.62, pred[]{:T(512)S(6)} %lt.168), kind=kOutput, calls=%fused_computation.1.clone.1 | convolution fusion | flops 201457664 | bytes 2097157 | tf_op jit(solution)/shard_map/while/body/eval_jaxpr/hde,hef->hdf/dot_general | solution.py:110
  139.4 2.1 %fusion.247 = f32[8,128,128]{1,2,0:T(8,128)S(1)} fusion(f32[8,128,128]{1,2,0:T(8,128)S(1)} %copy.69, f32[8,8,128,128]{3,2,1,0:T(8,128)} %get-tuple-element.154, s32[]{:T(128)S(6)} %copy.62, pred[]{:T(512)S(6)} %lt.168), kind=kOutput, calls=%fused_computation.1.clone.1 | convolution fusion | flops 201457664 | bytes 2097157 | tf_op jit(solution)/shard_map/while/body/eval_jaxpr/hde,hef->hdf/dot_general | solution.py:110
  141.5 2.1 %fusion.247 = f32[8,128,128]{1,2,0:T(8,128)S(1)} fusion(f32[8,128,128]{1,2,0:T(8,128)S(1)} %copy.69, f32[8,8,128,128]{3,2,1,0:T(8,128)} %get-tuple-element.154, s32[]{:T(128)S(6)} %copy.62, pred[]{:T(512)S(6)} %lt.168), kind=kOutput, calls=%fused_computation.1.clone.1 | convolution fusion | flops 201457664 | bytes 2097157 | tf_op jit(solution)/shard_map/while/body/eval_jaxpr/hde,hef->hdf/dot_general | solution.py:110
  143.7 2.1 %fusion.247 = f32[8,128,128]{1,2,0:T(8,128)S(1)} fusion(f32[8,128,128]{1,2,0:T(8,128)S(1)} %copy.69, f32[8,8,128,128]{3,2,1,0:T(8,128)} %get-tuple-element.154, s32[]{:T(128)S(6)} %copy.62, pred[]{:T(512)S(6)} %lt.168), kind=kOutput, calls=%fused_computation.1.clone.1 | convolution fusion | flops 201457664 | bytes 2097157 | tf_op jit(solution)/shard_map/while/body/eval_jaxpr/hde,hef->hdf/dot_general | solution.py:110
  145.7 1.1 fusion.8
  147.0 0.9 copy.50
  147.8 0.8 copy.49
  (90 shorter events, 13.3 us)
Async XLA Ops:
  7.2 21.9 %all-gather.4.cloned.1.call-start = ((), (), s32[]{:S(2)}) async-start(), calls=%async_computation | async-start | bytes 1310720 | tf_op jit(solution)/shard_map/all_gather | solution.py:75
  7.9 120.7 %all-gather.6.cloned.1.call-start = ((), (), s32[]{:S(2)}) async-start(), calls=%async_computation.1 | async-start | bytes 4718592 | tf_op jit(solution)/shard_map/all_gather | solution.py:11
  10.6 40.3 %copy-start = (bf16[128,8,128]{2,0,1:T(8,128)(2,1)}, bf16[128,8,128]{2,0,1:T(8,128)(2,1)S(1)}, u32[]{:S(2)}) copy-start(bf16[128,8,128]{2,0,1:T(8,128)(2,1)S(1)} %copy.41) | copy-start | bytes 786436
Sparse Core Ops, SparseCore 0:
  9.6 19.4 all-gather.3
  55.2 73.3 all-gather.5
where the time goes:
time: 156 us
  waiting for transfers between devices  89.6 us (57%)
  matrix products  44.8 us (29%)
  between operations  14.7 us (9%)
  local copies, waits for them, and re-layouts  5.25 us (3%)
    all_gather x1, waiting for transfers between devices, entering(): everything = lax.all_gather(array, axis)  70.6 us
    all_gather x1, waiting for transfers between devices, body(): lax.all_gather(features, 'head', axis=1, tiled=True)  18.3 us
    dot_general x8, matrix products, combine(): return jnp.einsum('hde,hef->hdf', earlier, later, precision=highest)  16.5 us
    dot_general x24, matrix products, small_inverse(): power = jnp.einsum('hij,hjk->hik', power, power, precision=highest)  5.1 us
    dot_general x24, matrix products, small_inverse(): jnp.einsum('hij,hjk->hik', result, power, precision=highest)  5.05 us
    dot_general x1, matrix products, body(): jnp.dot(lax.all_gather(features, 'head', axis=1, tiled=True), proj_weight...  4.97 us
    unnamed x8, local copies, waits for them, and re-layouts  4.13 us
  transfers between devices with their start and end apart: 2, of which 2 were waited for; matrix products, arithmetic and copies ran while one was open for 4% of the time, Pallas kernels for 0%

commit v1 on v0

v1 whole, which is shorter than its diff:
```python
import functools

import jax
import jax.numpy as jnp
from jax import lax
from jax.experimental import pallas as pl
from jax.experimental.pallas import tpu as pltpu
from jax.sharding import PartitionSpec as P

HEAD_DIM = 128
CHUNKS = 2
MESH = pl.DeviceIdType.MESH
F32 = jnp.float32
BF16 = jnp.bfloat16


def split(x):
    hi = x.astype(BF16)
    return hi, (x - hi.astype(F32)).astype(BF16)


def left_of(x):
    return jnp.concatenate(split(x), axis=1)


def right_of(x):
    row = jnp.concatenate(split(x), axis=1)
    return jnp.concatenate([row, row], axis=0)


def fold(r):
    half = r.shape[1] // 2
    return r[:, :half] + r[:, half:]


def product(left, right):
    return fold(jnp.dot(left, right, preferred_element_type=F32))


def product_t(left, right):
    return fold(lax.dot_general(left, right, (((1,), (1,)), ((), ())), preferred_element_type=F32))


def mm(a, b):
    return product(left_of(a), right_of(b))


def kernel(
    n_seq, feat_ref, w_hbm, q_ref, k_ref, oq_ref, ok_ref,
    w_buf, near, far, across, acc, w_dir, v_buf, local, pair, ct, chain, toward, other, outgoing,
    w_sem, gs_sem, gr_sem, s_sem, r_sem,
):
    seq, head = lax.axis_index("seq"), lax.axis_index("head")
    n_pairs = n_seq // 2
    x = seq % 2
    z = seq // 2
    partner = seq + 1 - 2 * x
    sibling = head + 1 - 2 * (head % 2)
    opposite = (head + 2) % 4
    diagonal = (sibling + 2) % 4
    tok, depth = feat_ref.shape
    heads = acc.shape[0]
    half = heads // 2
    piece = depth // CHUNKS
    dim = HEAD_DIM

    loads = []
    for j, owner in enumerate((head, sibling, opposite, diagonal)):
        load = pltpu.make_async_copy(
            w_hbm.at[pl.ds(pl.multiple_of(owner * depth, depth), depth), :], w_buf.at[j], w_sem.at[j]
        )
        load.start()
        loads.append(load)

    barrier = pltpu.get_barrier_semaphore()
    for target in ({"seq": partner}, {"head": sibling}, {"head": opposite}):
        pl.semaphore_signal(barrier, inc=1, device_id=target, device_id_type=MESH)

    @pl.when(z < n_pairs - 1)
    def _():
        pl.semaphore_signal(barrier, inc=1, device_id={"seq": seq + 2}, device_id_type=MESH)

    @pl.when(z > 0)
    def _():
        pl.semaphore_signal(barrier, inc=1, device_id={"seq": seq - 2}, device_id_type=MESH)

    both = jnp.where(z > 0, 1, 0) + jnp.where(z < n_pairs - 1, 1, 0)
    pl.semaphore_wait(barrier, 3 + both)

    def remote(src, dst, send, recv, target):
        return pltpu.make_async_remote_copy(
            src_ref=src, dst_ref=dst, send_sem=send, recv_sem=recv, device_id=target, device_id_type=MESH
        )

    to_far = []
    for c in range(CHUNKS):
        copy = remote(
            feat_ref.at[:, c * piece:(c + 1) * piece], far.at[c], gs_sem.at[1 + c], gr_sem.at[1 + c], {"head": opposite}
        )
        copy.start()
        to_far.append(copy)
    to_near = remote(feat_ref, near, gs_sem.at[0], gr_sem.at[0], {"head": sibling})
    to_near.start()

    def project(block, rows, first=False):
        for n in range(heads // 2):
            columns = slice(n * 2 * dim, (n + 1) * 2 * dim)
            part = jnp.dot(block, rows[:, columns], preferred_element_type=F32)
            for m in range(2):
                value = part[:, m * dim:(m + 1) * dim]
                if first:
                    acc[2 * n + m] = value
                else:
                    acc[2 * n + m] += value

    loads[0].wait()
    project(feat_ref[...], w_buf.at[0], True)
    loads[1].wait()
    to_near.wait_recv()
    project(near[...], w_buf.at[1])
    loads[2].wait()
    loads[3].wait()
    to_across = []
    for c in range(CHUNKS):
        to_far[c].wait_recv()
        copy = remote(far.at[c], across.at[c], gs_sem.at[1 + CHUNKS + c], gr_sem.at[1 + CHUNKS + c], {"head": sibling})
        copy.start()
        to_across.append(copy)
        rows = pl.ds(c * piece, piece)
        project(far[c], w_buf.at[2, rows])
        copy.wait_recv()
        project(across[c], w_buf.at[3, rows])

    i_pos = lax.broadcasted_iota(jnp.int32, (tok, tok), 0)
    j_pos = lax.broadcasted_iota(jnp.int32, (tok, tok), 1)
    eye = jnp.where(i_pos == j_pos, 1.0, 0.0).astype(F32)

    def group(g, at_end):
        ws, grams, inverses = [], [], []
        for i in range(half):
            raw = acc[g * half + i]
            w = raw * lax.rsqrt(jnp.sum(raw * raw, axis=-1, keepdims=True) + 1e-06)
            w_dir[g * half + i] = w
            ws.append(w)
        for w in ws:
            hi, lo = split(w)
            right = jnp.concatenate(
                [jnp.concatenate([hi, hi], axis=1), jnp.concatenate([lo, lo], axis=1)], axis=0
            )
            grams.append(product_t(jnp.concatenate([hi, lo], axis=1), right))
        size = 1
        while size < tok:
            mask = (i_pos // (2 * size) == j_pos // (2 * size)) & (i_pos // size > j_pos // size)
            if size == 1:
                inverses = [2.0 * eye - 4.0 * jnp.where(mask, gram, 0.0) for gram in grams]
            else:
                rights = [right_of(inv) for inv in inverses]
                middles = [
                    product(left_of(jnp.where(mask, gram, 0.0)), right) for gram, right in zip(grams, rights)
                ]
                inverses = [inv - mm(inv, middle) for inv, middle in zip(inverses, middles)]
            size *= 2
        vs = [mm(inv, w) for inv, w in zip(inverses, ws)]
        for i in range(half):
            v_buf[g * half + i] = vs[i]
            at_end(i, eye - mm(ws[i].T, vs[i]))

    first = []
    for i in range(half):
        first.append(remote(outgoing.at[i], pair.at[x, i], s_sem.at[0, i], r_sem.at[0, i], {"seq": partner}))

    def send_off(i, value):
        outgoing[i] = value
        first[i].start()

    def keep(i, value):
        pair[x, i] = value

    group(1 - x, send_off)
    group(x, keep)

    below = lax.broadcasted_iota(jnp.int32, (2 * tok, tok), 0) % tok >= lax.broadcasted_iota(jnp.int32, (2 * tok, tok), 1)
    for hh in range(heads):
        columns = slice(hh * dim, (hh + 1) * dim)
        targets = jnp.concatenate([q_ref[:, columns], k_ref[:, columns]], axis=0)
        along = product_t(targets, jnp.concatenate(split(w_dir[hh]), axis=0))
        local[hh] = left_of(targets.astype(F32) - mm(jnp.where(below, along, 0.0), v_buf[hh]))

    chained, last = [], []
    for i in range(half):
        chained.append(remote(ct.at[i], chain.at[i], s_sem.at[1, i], r_sem.at[1, i], {"seq": seq + 2}))
        last.append(remote(toward.at[i], other.at[i], s_sem.at[2, i], r_sem.at[2, i], {"seq": partner}))

    @pl.when(z == 0)
    def _():
        for i in range(half):
            chain[i] = eye

    for i in range(half):
        pltpu.make_async_remote_copy(
            src_ref=outgoing.at[i], dst_ref=pair.at[1 - x, i], send_sem=s_sem.at[0, i], recv_sem=r_sem.at[0, i],
            device_id={"seq": partner}, device_id_type=MESH,
        ).wait_recv()
        ct[i] = mm(pair[1, i], pair[0, i])

    for i in range(half):
        @pl.when(z > 0)
        def _():
            chained[i].wait_recv()

            @pl.when(z < n_pairs - 1)
            def _():
                ct[i] = mm(ct[i], chain[i])

        @pl.when(z < n_pairs - 1)
        def _():
            chained[i].start()

        even = chain[i]
        odd = mm(pair[0, i], even)
        toward[i] = jnp.where(x == 0, odd, even)
        last[i].start()
        mine = jnp.where(x == 0, even, odd)
        finish(x * half + i, mine, local, oq_ref, ok_ref)

    for i in range(half):
        last[i].wait_recv()
        finish((1 - x) * half + i, other[i], local, oq_ref, ok_ref)

    to_near.wait_send()
    for c in range(CHUNKS):
        to_far[c].wait_send()
        to_across[c].wait_send()
    for i in range(half):
        first[i].wait_send()
        last[i].wait_send()

    @pl.when(z < n_pairs - 1)
    def _():
        for i in range(half):
            chained[i].wait_send()


def finish(hh, entering, local, oq_ref, ok_ref):
    tok = oq_ref.shape[0]
    out = product(local[hh], right_of(entering)).astype(BF16)
    columns = pl.ds(pl.multiple_of(hh * HEAD_DIM, HEAD_DIM), HEAD_DIM)
    oq_ref[:, columns] = out[:tok]
    ok_ref[:, columns] = out[tok:]


def solution(mesh):
    n_seq = mesh.shape["seq"]

    def body(features, proj_weight, query_vectors, key_vectors):
        tok, depth = features.shape
        width = proj_weight.shape[1]
        heads = width // HEAD_DIM
        half = heads // 2
        square = (HEAD_DIM, HEAD_DIM)
        vmem = pl.BlockSpec(memory_space=pltpu.VMEM)
        out = jax.ShapeDtypeStruct((tok, width), BF16)
        return pl.pallas_call(
            functools.partial(kernel, n_seq),
            out_shape=(out, out),
            in_specs=[vmem, pl.BlockSpec(memory_space=pl.ANY), vmem, vmem],
            out_specs=(vmem, vmem),
            scratch_shapes=[
                pltpu.VMEM((4, depth, width), BF16),
                pltpu.VMEM((tok, depth), BF16),
                pltpu.VMEM((CHUNKS, tok, depth // CHUNKS), BF16),
                pltpu.VMEM((CHUNKS, tok, depth // CHUNKS), BF16),
                pltpu.VMEM((heads, tok, HEAD_DIM), F32),
                pltpu.VMEM((heads, tok, HEAD_DIM), F32),
                pltpu.VMEM((heads, tok, HEAD_DIM), F32),
                pltpu.VMEM((heads, 2 * tok, 2 * HEAD_DIM), BF16),
                pltpu.VMEM((2, half) + square, F32),
                pltpu.VMEM((half,) + square, F32),
                pltpu.VMEM((half,) + square, F32),
                pltpu.VMEM((half,) + square, F32),
                pltpu.VMEM((half,) + square, F32),
                pltpu.VMEM((half,) + square, F32),
                pltpu.SemaphoreType.DMA((4,)),
                pltpu.SemaphoreType.DMA((1 + 2 * CHUNKS,)),
                pltpu.SemaphoreType.DMA((1 + 2 * CHUNKS,)),
                pltpu.SemaphoreType.DMA((3, half)),
                pltpu.SemaphoreType.DMA((3, half)),
            ],
            compiler_params=pltpu.CompilerParams(
                collective_id=0, has_side_effects=True, vmem_limit_bytes=56 * 1024 * 1024
            ),
            cost_estimate=pl.CostEstimate(flops=4_000_000_000, bytes_accessed=10_000_000, transcendentals=0),
        )(features, proj_weight, query_vectors, key_vectors)

    in_specs = (P("seq", "head"), P(None, "head"), P("seq", "head"), P("seq", "head"))
    out_specs = (P("seq", "head"), P("seq", "head"))
    return jax.shard_map(body, mesh=mesh, in_specs=in_specs, out_specs=out_specs, check_vma=False)
```

time: 156 us -> 44.5 us (0.29)
  the two profiles are of different devices: /device:TPU:0 before, /device:TPU:24 now
where the time goes in v1:
time: 44.5 us; the launch traced here: 44.3 us
  Pallas kernels  40.4 us (91%)
  local copies, waits for them, and re-layouts  3.34 us (8%)
  between operations  0.64 us (1%)
    pallas_call x1, Pallas kernels, body(): pl.pallas_call(functools.partial(kernel, n_seq), out_shape=(out, out), in...  40.4 us
    unnamed x2, local copies, waits for them, and re-layouts  3.34 us

profile of v1, /device:TPU:24, one launch (start us, length us, event | category | flops | bytes accessed | tf_op | source)
XLA Modules:
  0.0 44.3 jit_solution(768752435163816587)
XLA Ops:
  0.6 40.4 %shard_map.59 = (bf16[128,1024]{1,0:T(8,128)(2,1)}, bf16[128,1024]{1,0:T(8,128)(2,1)}) custom-call(bf16[128,1024]{1,0:T(8,128)(2,1)} %feat_ref.1, bf16[4096,1024]{1,0:T(8,128)(2,1)} %w_hbm.1, bf16[128,1024]{1,0:T(8,128)(2,1)} %q_ref.1, bf16[128,1024]{1,0:T(8,128)(2,1)} %k_ref.1), custom_call_target="tpu_custom_call" | custom-call | flops 4000000000 | bytes 10000000 | tf_op jit(solution)/shard_map/pallas_call | solution.py:263
  41.0 1.7 %copy.8 = bf16[128,1024]{1,0:T(8,128)(2,1)} copy(bf16[128,1024]{1,0:T(8,128)(2,1)} %get-tuple-element.4) | data formatting | bytes 524288
  42.7 1.7 %copy.9 = bf16[128,1024]{1,0:T(8,128)(2,1)} copy(bf16[128,1024]{1,0:T(8,128)(2,1)} %get-tuple-element.5) | data formatting | bytes 524288

commit v2 on v1

--- a/solution.py
+++ b/solution.py
@@ -46,8 +46,8 @@
 
 
 def kernel(
-    n_seq, feat_ref, w_hbm, q_ref, k_ref, oq_ref, ok_ref,
-    w_buf, near, far, across, acc, w_dir, v_buf, local, pair, ct, chain, toward, other, outgoing,
+    n_seq, feat_hbm, w_hbm, q_hbm, k_hbm, out_ref,
+    feat_ref, x_ref, w_buf, near, far, across, acc, w_dir, v_buf, local, pair, ct, chain, toward, other, outgoing,
     w_sem, gs_sem, gr_sem, s_sem, r_sem,
 ):
     seq, head = lax.axis_index("seq"), lax.axis_index("head")
@@ -58,12 +58,14 @@
     sibling = head + 1 - 2 * (head % 2)
     opposite = (head + 2) % 4
     diagonal = (sibling + 2) % 4
-    tok, depth = feat_ref.shape
+    tok, depth = feat_hbm.shape
     heads = acc.shape[0]
     half = heads // 2
     piece = depth // CHUNKS
     dim = HEAD_DIM
 
+    feat_load = pltpu.make_async_copy(feat_hbm, feat_ref, w_sem.at[4])
+    feat_load.start()
     loads = []
     for j, owner in enumerate((head, sibling, opposite, diagonal)):
         load = pltpu.make_async_copy(
@@ -71,6 +73,10 @@
         )
         load.start()
         loads.append(load)
+    q_load = pltpu.make_async_copy(q_hbm, x_ref.at[:tok], w_sem.at[5])
+    k_load = pltpu.make_async_copy(k_hbm, x_ref.at[tok:], w_sem.at[6])
+    q_load.start()
+    k_load.start()
 
     barrier = pltpu.get_barrier_semaphore()
     for target in ({"seq": partner}, {"head": sibling}, {"head": opposite}):
@@ -95,11 +101,11 @@
     to_far = []
     for c in range(CHUNKS):
         copy = remote(
-            feat_ref.at[:, c * piece:(c + 1) * piece], far.at[c], gs_sem.at[1 + c], gr_sem.at[1 + c], {"head": opposite}
+            feat_hbm.at[:, c * piece:(c + 1) * piece], far.at[c], gs_sem.at[1 + c], gr_sem.at[1 + c], {"head": opposite}
         )
         copy.start()
         to_far.append(copy)
-    to_near = remote(feat_ref, near, gs_sem.at[0], gr_sem.at[0], {"head": sibling})
+    to_near = remote(feat_hbm, near, gs_sem.at[0], gr_sem.at[0], {"head": sibling})
     to_near.start()
 
     def project(block, rows, first=False):
@@ -113,6 +119,7 @@
                 else:
                     acc[2 * n + m] += value
 
+    feat_load.wait()
     loads[0].wait()
     project(feat_ref[...], w_buf.at[0], True)
     loads[1].wait()
@@ -135,12 +142,12 @@
     j_pos = lax.broadcasted_iota(jnp.int32, (tok, tok), 1)
     eye = jnp.where(i_pos == j_pos, 1.0, 0.0).astype(F32)
 
-    def group(g, at_end):
+    def group(start, count, at_end):
         ws, grams, inverses = [], [], []
-        for i in range(half):
-            raw = acc[g * half + i]
+        for i in range(count):
+            raw = acc[start + i]
             w = raw * lax.rsqrt(jnp.sum(raw * raw, axis=-1, keepdims=True) + 1e-06)
-            w_dir[g * half + i] = w
+            w_dir[start + i] = w
             ws.append(w)
         for w in ws:
             hi, lo = split(w)
@@ -161,8 +168,8 @@
                 inverses = [inv - mm(inv, middle) for inv, middle in zip(inverses, middles)]
             size *= 2
         vs = [mm(inv, w) for inv, w in zip(inverses, ws)]
-        for i in range(half):
-            v_buf[g * half + i] = vs[i]
+        for i in range(count):
+            v_buf[start + i] = vs[i]
             at_end(i, eye - mm(ws[i].T, vs[i]))
 
     first = []
@@ -176,13 +183,22 @@
     def keep(i, value):
         pair[x, i] = value
 
-    group(1 - x, send_off)
-    group(x, keep)
-
+    def done(i, value):
+        @pl.when((i // half) == x)
+        def _():
+            pair[x, i % half] = value
+        @pl.when((i // half) != x)
+        def _():
+            outgoing[i % half] = value
+            first[i % half].start()
+    group(0, heads, done)
+
+    q_load.wait()
+    k_load.wait()
     below = lax.broadcasted_iota(jnp.int32, (2 * tok, tok), 0) % tok >= lax.broadcasted_iota(jnp.int32, (2 * tok, tok), 1)
     for hh in range(heads):
         columns = slice(hh * dim, (hh + 1) * dim)
-        targets = jnp.concatenate([q_ref[:, columns], k_ref[:, columns]], axis=0)
+        targets = x_ref[:, columns]
         along = product_t(targets, jnp.concatenate(split(w_dir[hh]), axis=0))
         local[hh] = left_of(targets.astype(F32) - mm(jnp.where(below, along, 0.0), v_buf[hh]))
 
@@ -197,13 +213,9 @@
             chain[i] = eye
 
     for i in range(half):
-        pltpu.make_async_remote_copy(
-            src_ref=outgoing.at[i], dst_ref=pair.at[1 - x, i], send_sem=s_sem.at[0, i], recv_sem=r_sem.at[0, i],
-            device_id={"seq": partner}, device_id_type=MESH,
-        ).wait_recv()
+        remote(outgoing.at[i], pair.at[1 - x, i], s_sem.at[0, i], r_sem.at[0, i], {"seq": partner}).wait_recv()
         ct[i] = mm(pair[1, i], pair[0, i])
 
-    for i in range(half):
         @pl.when(z > 0)
         def _():
             chained[i].wait_recv()
@@ -216,16 +228,22 @@
         def _():
             chained[i].start()
 
-        even = chain[i]
-        odd = mm(pair[0, i], even)
-        toward[i] = jnp.where(x == 0, odd, even)
+        @pl.when(x == 0)
+        def _():
+            toward[i] = mm(pair[0, i], chain[i])
+
+        @pl.when(x == 1)
+        def _():
+            toward[i] = chain[i]
+            chain[i] = mm(pair[0, i], chain[i])
+
         last[i].start()
-        mine = jnp.where(x == 0, even, odd)
-        finish(x * half + i, mine, local, oq_ref, ok_ref)
-
+
+    for i in range(half):
+        finish(x * half + i, chain[i], local, out_ref)
     for i in range(half):
         last[i].wait_recv()
-        finish((1 - x) * half + i, other[i], local, oq_ref, ok_ref)
+        finish((1 - x) * half + i, other[i], local, out_ref)
 
     to_near.wait_send()
     for c in range(CHUNKS):
@@ -241,12 +259,16 @@
             chained[i].wait_send()
 
 
-def finish(hh, entering, local, oq_ref, ok_ref):
-    tok = oq_ref.shape[0]
+def finish(hh, entering, local, out_ref):
     out = product(local[hh], right_of(entering)).astype(BF16)
     columns = pl.ds(pl.multiple_of(hh * HEAD_DIM, HEAD_DIM), HEAD_DIM)
-    oq_ref[:, columns] = out[:tok]
-    ok_ref[:, columns] = out[tok:]
+    out_ref[:, columns] = out
+
+
+def part(both_ref, q_ref, k_ref):
+    tok = q_ref.shape[0]
+    q_ref[...] = both_ref[:tok]
+    k_ref[...] = both_ref[tok:]
 
 
 def solution(mesh):
@@ -260,12 +282,14 @@
         square = (HEAD_DIM, HEAD_DIM)
         vmem = pl.BlockSpec(memory_space=pltpu.VMEM)
         out = jax.ShapeDtypeStruct((tok, width), BF16)
-        return pl.pallas_call(
+        both = pl.pallas_call(
             functools.partial(kernel, n_seq),
-            out_shape=(out, out),
-            in_specs=[vmem, pl.BlockSpec(memory_space=pl.ANY), vmem, vmem],
-            out_specs=(vmem, vmem),
+            out_shape=jax.ShapeDtypeStruct((2 * tok, width), BF16),
+            in_specs=[pl.BlockSpec(memory_space=pl.ANY)] * 4,
+            out_specs=vmem,
             scratch_shapes=[
+                pltpu.VMEM((tok, depth), BF16),
+                pltpu.VMEM((2 * tok, width), BF16),
                 pltpu.VMEM((4, depth, width), BF16),
                 pltpu.VMEM((tok, depth), BF16),
                 pltpu.VMEM((CHUNKS, tok, depth // CHUNKS), BF16),
@@ -280,7 +304,7 @@
                 pltpu.VMEM((half,) + square, F32),
                 pltpu.VMEM((half,) + square, F32),
                 pltpu.VMEM((half,) + square, F32),
-                pltpu.SemaphoreType.DMA((4,)),
+                pltpu.SemaphoreType.DMA((7,)),
                 pltpu.SemaphoreType.DMA((1 + 2 * CHUNKS,)),
                 pltpu.SemaphoreType.DMA((1 + 2 * CHUNKS,)),
                 pltpu.SemaphoreType.DMA((3, half)),
@@ -291,6 +315,7 @@
             ),
             cost_estimate=pl.CostEstimate(flops=4_000_000_000, bytes_accessed=10_000_000, transcendentals=0),
         )(features, proj_weight, query_vectors, key_vectors)
+        return pl.pallas_call(part, out_shape=(out, out), in_specs=[vmem], out_specs=(vmem, vmem))(both)
 
     in_specs = (P("seq", "head"), P(None, "head"), P("seq", "head"), P("seq", "head"))
     out_specs = (P("seq", "head"), P("seq", "head"))

time: 44.5 us -> 38.6 us (0.87)
  local copies, waits for them, and re-layouts: 3.34 us -> 0 us
  Pallas kernels: 40.4 us -> 37.8 us
    unnamed x2 -> x0, local copies, waits for them, and re-layouts: 3.34 us -> none
    pallas_call x1 -> x2, Pallas kernels: 40.4 us -> 37.8 us  [the longest x1 35.9 us: body(): pl.pallas_call(functools.partial(kernel, n_seq), out_shape=jax.ShapeDtype...]
where the time goes in v2:
time: 38.6 us; the launch traced here: 38.4 us
  Pallas kernels  37.8 us (98%)
  between operations  0.64 us (2%)
    pallas_call x1, Pallas kernels, body(): pl.pallas_call(functools.partial(kernel, n_seq), out_shape=jax.ShapeDtype...  35.9 us
    pallas_call x1, Pallas kernels, body(): pl.pallas_call(part, out_shape=(out, out), in_specs=[vmem], out_specs=(vm...  1.85 us

profile of v2, /device:TPU:24, one launch (start us, length us, event | category | flops | bytes accessed | tf_op | source)
XLA Modules:
  0.0 38.4 jit_solution(15035582125791262002)
XLA Ops:
  0.6 35.9 %shard_map.59.both_ref = bf16[256,1024]{1,0:T(8,128)(2,1)} custom-call(bf16[128,1024]{1,0:T(8,128)(2,1)} %feat_hbm.1, bf16[4096,1024]{1,0:T(8,128)(2,1)} %w_hbm.1, bf16[128,1024]{1,0:T(8,128)(2,1)} %q_hbm.1, bf16[128,1024]{1,0:T(8,128)(2,1)} %k_hbm.1), custom_call_target="tpu_custom_call" | custom-call | flops 4000000000 | bytes 10000000 | tf_op jit(solution)/shard_map/pallas_call | solution.py:285
  36.6 1.8 %shard_map.60 = (bf16[128,1024]{1,0:T(8,128)(2,1)}, bf16[128,1024]{1,0:T(8,128)(2,1)}) custom-call(bf16[256,1024]{1,0:T(8,128)(2,1)} %shard_map.59.both_ref), custom_call_target="tpu_custom_call" | custom-call | tf_op jit(solution)/shard_map/pallas_call | solution.py:318

commit v3 on v2

--- a/solution.py
+++ b/solution.py
@@ -9,6 +9,7 @@
 
 HEAD_DIM = 128
 CHUNKS = 2
+CUTS = 2
 MESH = pl.DeviceIdType.MESH
 F32 = jnp.float32
 BF16 = jnp.bfloat16
@@ -47,7 +48,7 @@
 
 def kernel(
     n_seq, feat_hbm, w_hbm, q_hbm, k_hbm, out_ref,
-    feat_ref, x_ref, w_buf, near, far, across, acc, w_dir, v_buf, local, pair, ct, chain, toward, other, outgoing,
+    feat_ref, x_ref, w_buf, near, far, across, acc, w_dir, v_buf, local, pair, ct, chain, toward, other, outgoing, mine,
     w_sem, gs_sem, gr_sem, s_sem, r_sem,
 ):
     seq, head = lax.axis_index("seq"), lax.axis_index("head")
@@ -170,7 +171,7 @@
         vs = [mm(inv, w) for inv, w in zip(inverses, ws)]
         for i in range(count):
             v_buf[start + i] = vs[i]
-            at_end(i, eye - mm(ws[i].T, vs[i]))
+            at_end(i, eye - mm(vs[i].T, ws[i]))
 
     first = []
     for i in range(half):
@@ -202,10 +203,12 @@
         along = product_t(targets, jnp.concatenate(split(w_dir[hh]), axis=0))
         local[hh] = left_of(targets.astype(F32) - mm(jnp.where(below, along, 0.0), v_buf[hh]))
 
+    rows = tok // CUTS
+    pieces = [(i, pl.ds(r * rows, rows)) for i in range(half) for r in range(CUTS)]
     chained, last = [], []
-    for i in range(half):
-        chained.append(remote(ct.at[i], chain.at[i], s_sem.at[1, i], r_sem.at[1, i], {"seq": seq + 2}))
-        last.append(remote(toward.at[i], other.at[i], s_sem.at[2, i], r_sem.at[2, i], {"seq": partner}))
+    for p, (i, cut) in enumerate(pieces):
+        chained.append(remote(ct.at[i, cut], chain.at[i, cut], s_sem.at[1, p], r_sem.at[1, p], {"seq": seq + 2}))
+        last.append(remote(toward.at[i, cut], other.at[i, cut], s_sem.at[2, p], r_sem.at[2, p], {"seq": partner}))
 
     @pl.when(z == 0)
     def _():
@@ -214,35 +217,34 @@
 
     for i in range(half):
         remote(outgoing.at[i], pair.at[1 - x, i], s_sem.at[0, i], r_sem.at[0, i], {"seq": partner}).wait_recv()
-        ct[i] = mm(pair[1, i], pair[0, i])
-
-        @pl.when(z > 0)
-        def _():
-            chained[i].wait_recv()
+        even = right_of(pair[0, i])
+        step = jnp.concatenate([right_of(product(left_of(pair[0, i]), right_of(pair[1, i]))), even], axis=1)
+        for r in range(CUTS):
+            p = i * CUTS + r
+            cut = pieces[p][1]
+
+            @pl.when(z > 0)
+            def _():
+                chained[p].wait_recv()
+
+            before = chain[i, cut]
+            after = jnp.dot(left_of(before), step, preferred_element_type=F32)
+            ct[i, cut] = fold(after[:, :2 * dim])
 
             @pl.when(z < n_pairs - 1)
             def _():
-                ct[i] = mm(ct[i], chain[i])
-
-        @pl.when(z < n_pairs - 1)
-        def _():
-            chained[i].start()
-
-        @pl.when(x == 0)
-        def _():
-            toward[i] = mm(pair[0, i], chain[i])
-
-        @pl.when(x == 1)
-        def _():
-            toward[i] = chain[i]
-            chain[i] = mm(pair[0, i], chain[i])
-
-        last[i].start()
-
-    for i in range(half):
-        finish(x * half + i, chain[i], local, out_ref)
-    for i in range(half):
-        last[i].wait_recv()
+                chained[p].start()
+
+            odd = fold(after[:, 2 * dim:])
+            toward[i, cut] = jnp.where(x == 0, odd, before)
+            last[p].start()
+            mine[i, cut] = jnp.where(x == 0, before, odd)
+
+    for i in range(half):
+        finish(x * half + i, mine[i], local, out_ref)
+    for i in range(half):
+        for r in range(CUTS):
+            last[i * CUTS + r].wait_recv()
         finish((1 - x) * half + i, other[i], local, out_ref)
 
     to_near.wait_send()
@@ -251,16 +253,19 @@
         to_across[c].wait_send()
     for i in range(half):
         first[i].wait_send()
-        last[i].wait_send()
+    for copy in last:
+        copy.wait_send()
 
     @pl.when(z < n_pairs - 1)
     def _():
-        for i in range(half):
-            chained[i].wait_send()
+        for copy in chained:
+            copy.wait_send()
 
 
 def finish(hh, entering, local, out_ref):
-    out = product(local[hh], right_of(entering)).astype(BF16)
+    hi, lo = split(entering)
+    both = jnp.concatenate([jnp.concatenate([hi, hi], axis=1), jnp.concatenate([lo, lo], axis=1)], axis=0)
+    out = product_t(local[hh], both).astype(BF16)
     columns = pl.ds(pl.multiple_of(hh * HEAD_DIM, HEAD_DIM), HEAD_DIM)
     out_ref[:, columns] = out
 
@@ -304,11 +309,12 @@
                 pltpu.VMEM((half,) + square, F32),
                 pltpu.VMEM((half,) + square, F32),
                 pltpu.VMEM((half,) + square, F32),
+                pltpu.VMEM((half,) + square, F32),
                 pltpu.SemaphoreType.DMA((7,)),
                 pltpu.SemaphoreType.DMA((1 + 2 * CHUNKS,)),
                 pltpu.SemaphoreType.DMA((1 + 2 * CHUNKS,)),
-                pltpu.SemaphoreType.DMA((3, half)),
-                pltpu.SemaphoreType.DMA((3, half)),
+                pltpu.SemaphoreType.DMA((3, half * CUTS)),
+                pltpu.SemaphoreType.DMA((3, half * CUTS)),
             ],
             compiler_params=pltpu.CompilerParams(
                 collective_id=0, has_side_effects=True, vmem_limit_bytes=56 * 1024 * 1024

time: 38.6 us -> 37.8 us (0.979)
  Pallas kernels: 37.8 us -> 37 us
    pallas_call x1, Pallas kernels: 35.9 us -> 35.1 us  [body(): pl.pallas_call(functools.partial(kernel, n_seq), out_shape=jax.ShapeDtype...]
where the time goes in v3:
time: 37.8 us; the launch traced here: 37.6 us
  Pallas kernels  37 us (98%)
  between operations  0.64 us (2%)
    pallas_call x1, Pallas kernels, body(): pl.pallas_call(functools.partial(kernel, n_seq), out_shape=jax.ShapeDtype...  35.1 us
    pallas_call x1, Pallas kernels, body(): pl.pallas_call(part, out_shape=(out, out), in_specs=[vmem], out_specs=(vm...  1.85 us

profile of v3, /device:TPU:24, one launch (start us, length us, event | category | flops | bytes accessed | tf_op | source)
XLA Modules:
  0.0 37.6 jit_solution(13501118133350860952)
XLA Ops:
  0.6 35.1 %shard_map.59.both_ref = bf16[256,1024]{1,0:T(8,128)(2,1)} custom-call(bf16[128,1024]{1,0:T(8,128)(2,1)} %feat_hbm.1, bf16[4096,1024]{1,0:T(8,128)(2,1)} %w_hbm.1, bf16[128,1024]{1,0:T(8,128)(2,1)} %q_hbm.1, bf16[128,1024]{1,0:T(8,128)(2,1)} %k_hbm.1), custom_call_target="tpu_custom_call" | custom-call | flops 4000000000 | bytes 10000000 | tf_op jit(solution)/shard_map/pallas_call | solution.py:290
  35.8 1.8 %shard_map.60 = (bf16[128,1024]{1,0:T(8,128)(2,1)}, bf16[128,1024]{1,0:T(8,128)(2,1)}) custom-call(bf16[256,1024]{1,0:T(8,128)(2,1)} %shard_map.59.both_ref), custom_call_target="tpu_custom_call" | custom-call | tf_op jit(solution)/shard_map/pallas_call | solution.py:324

commit v4 on v3

--- a/solution.py
+++ b/solution.py
@@ -9,7 +9,7 @@
 
 HEAD_DIM = 128
 CHUNKS = 2
-CUTS = 2
+CUTS = 4
 MESH = pl.DeviceIdType.MESH
 F32 = jnp.float32
 BF16 = jnp.bfloat16

time: 37.8 us -> 37.7 us (level)
  no operation moved by 1% of the time
where the time goes in v4:
time: 37.7 us; the launch traced here: 37.5 us
  Pallas kernels  36.9 us (98%)
  between operations  0.64 us (2%)
    pallas_call x1, Pallas kernels, body(): pl.pallas_call(functools.partial(kernel, n_seq), out_shape=jax.ShapeDtype...  35 us
    pallas_call x1, Pallas kernels, body(): pl.pallas_call(part, out_shape=(out, out), in_specs=[vmem], out_specs=(vm...  1.85 us

profile of v4, /device:TPU:24, one launch (start us, length us, event | category | flops | bytes accessed | tf_op | source)
XLA Modules:
  0.0 37.5 jit_solution(6037715483436989520)
XLA Ops:
  0.6 35.0 %shard_map.59.both_ref = bf16[256,1024]{1,0:T(8,128)(2,1)} custom-call(bf16[128,1024]{1,0:T(8,128)(2,1)} %feat_hbm.1, bf16[4096,1024]{1,0:T(8,128)(2,1)} %w_hbm.1, bf16[128,1024]{1,0:T(8,128)(2,1)} %q_hbm.1, bf16[128,1024]{1,0:T(8,128)(2,1)} %k_hbm.1), custom_call_target="tpu_custom_call" | custom-call | flops 4000000000 | bytes 10000000 | tf_op jit(solution)/shard_map/pallas_call | solution.py:290
  35.7 1.8 %shard_map.60 = (bf16[128,1024]{1,0:T(8,128)(2,1)}, bf16[128,1024]{1,0:T(8,128)(2,1)}) custom-call(bf16[256,1024]{1,0:T(8,128)(2,1)} %shard_map.59.both_ref), custom_call_target="tpu_custom_call" | custom-call | tf_op jit(solution)/shard_map/pallas_call | solution.py:324
